TPU v7x, 512 devices: a whole 4x4x16 slice. The times are simulated.
512 devices in a mesh: smp: 128 (over x_lo, z, y), par: 4 (over x_hi, core).
Axes of the slice: x: 4 (x_hi: 2, x_lo: 2; x = x_hi * 2 + x_lo), y: 4, z: 16, core: 2. Of those that a mesh axis runs over, the one named last changes fastest.
Arguments:
- derivatives: bfloat16 [10240, 2048], P('smp', 'par'), may hold values from -40 to 40
- epsilon: float32 [10240], P('smp'), may hold values from -6 to 6
Outputs:
- gram_tile: float32 [10240, 10240], P('smp', 'par')
- update: float32 [2048], P('par')
All inputs are finite; a program needn't handle non-finite values.
Results may differ from a plain program's by a relative error of at most 0.003.
Values may be sent and summed in bfloat16 or wider, within the bound.
A program may use at most 64 MiB of HBM per device.

v0:
```python
import math

import jax
import jax.numpy as jnp
from jax import lax
from jax.sharding import PartitionSpec as P


def shards(derivatives, epsilon):
    total_rows = derivatives.shape[0] * lax.axis_size("smp")
    factor = 1.0 / math.sqrt(total_rows)
    totals = lax.psum(jnp.sum(derivatives.astype(jnp.float32), axis=0), "smp")
    column_mean = totals / total_rows
    own_rows = ((derivatives.astype(jnp.float32) - column_mean) * factor).astype(jnp.bfloat16)
    partial_terms = jnp.dot(
        own_rows,
        lax.all_gather(own_rows, "smp", axis=0, tiled=True).T,
        preferred_element_type=jnp.float32,
    )
    gram_tile = lax.psum_scatter(partial_terms, "par", scatter_dimension=1, tiled=True)
    local_sum = jnp.dot(epsilon, own_rows.astype(jnp.float32), precision=lax.Precision.HIGHEST)
    update = lax.psum(local_sum, "smp")
    return (gram_tile, update)


def solution(mesh):
    in_specs = (P("smp", "par"), P("smp"))
    out_specs = (P("smp", "par"), P("par"))
    return jax.shard_map(shards, mesh=mesh, in_specs=in_specs, out_specs=out_specs, check_vma=False)
```

profile of v0, /device:TPU:24, one launch (start us, length us, event | category | flops | bytes accessed | tf_op | source)
XLA Modules:
  0.0 1238.4 jit_solution(3614393714561013606)
XLA Ops:
  7.2 0.0 copy-start
  7.2 0.0 all-gather.2.cloned.1.call-start
  7.2 0.9 convert_reduce_fusion
  8.1 306.2 %psum.14 = f32[512]{0:T(512)S(1)} all-reduce(f32[512]{0:T(512)S(1)} %convert_reduce_fusion), channel_id=1, replica_groups=mesh['smp'=128,'par'=4] {'smp'}, use_global_device_ids=true, to_apply=%region_1.0 | all-reduce | flops 512 | bytes 4096 | tf_op jit(solution)/shard_map/psum | solution.py:12
  314.3 1.5 fusion.1
  315.8 0.0 copy-start.1
  315.8 0.0 all-gather.2.cloned.1.call-update
  315.9 0.0 reduce-scatter.2.cloned.1.call-start
  315.9 602.9 %all-gather.2.cloned.1.call-done = bf16[10240,512]{1,0:T(8,128)(2,1)} async-done(((bf16[80,512]{1,0:T(8,128)(2,1)}), bf16[10240,512]{1,0:T(8,128)(2,1)}) %all-gather.2.cloned.1.call-update) | async-done | bytes 10485776 | tf_op jit(solution)/shard_map/all_gather | solution.py:17
  918.8 9.1 fusion.4
  927.9 0.0 reduce-scatter.2.cloned.1.call-update
  927.9 0.0 copy-done
  928.0 0.0 copy-done.1
  928.0 0.1 fusion.2
  928.1 303.5 %psum.15 = f32[512]{0:T(512)} all-reduce(f32[512]{0:T(512)S(1)} %bitcast.7), channel_id=1, replica_groups=mesh['smp'=128,'par'=4] {'smp'}, use_global_device_ids=true, to_apply=%region_3.0 | all-reduce | flops 512 | bytes 4096 | tf_op jit(solution)/shard_map/psum | solution.py:22
  1231.6 0.0 reduce-scatter.2.cloned.1.call-done
  (1 shorter events, 0.0 us)
Async XLA Ops:
  7.2 920.8 %copy-start = (f32[80]{0:T(128)S(1)}, f32[80]{0:T(128)}, u32[]{:S(2)}) copy-start(f32[80]{0:T(128)} %param.3) | copy-start | bytes 964
  7.2 911.7 %all-gather.2.cloned.1.call-start = ((), (), s32[]{:S(2)}) async-start(), calls=%async_computation.1 | async-start | bytes 10567680 | tf_op jit(solution)/shard_map/all_gather | solution.py:17
  315.8 612.1 %copy-start.1 = (bf16[80,512]{1,0:T(8,128)(2,1)S(1)}, bf16[80,512]{1,0:T(8,128)(2,1)}, u32[]{:S(2)}) copy-start(bf16[80,512]{1,0:T(8,128)(2,1)} %fusion.1) | copy-start | bytes 245764
  315.9 915.7 %reduce-scatter.2.cloned.1.call-start = ((), (), s32[]{:S(2)}) async-start(), calls=%async_computation.2 | async-start | bytes 4096000 | tf_op jit(solution)/shard_map/reduce_scatter | solution.py:20
Sparse Core Ops, SparseCore 0:
  316.0 602.8 all-gather.1
  928.1 55.4 reduce-scatter.1
where the time goes:
time: 1250 us; the launch traced here: 1240 us
  blocking collectives  610 us (49%)
  waiting for transfers between devices  603 us (48%)
  between operations  14.1 us (1%)
    all_gather x1, waiting for transfers between devices, shards(): lax.all_gather(own_rows, 'smp', axis=0, tiled=True)  603 us
    psum x1, blocking collectives, shards(): totals = lax.psum(jnp.sum(derivatives.astype(jnp.float32), axis=0), 'smp')  306 us
    psum x1, blocking collectives, shards(): update = lax.psum(local_sum, 'smp')  303 us
  transfers between devices with their start and end apart: 2, of which 1 were waited for; matrix products, arithmetic and copies ran while one was open for 0% of the time, Pallas kernels for 0%

commit v1 on v0

v1 whole, which is shorter than its diff:
```python
import functools
import math

import jax
import jax.numpy as jnp
from jax import lax
from jax.experimental import pallas as pl
from jax.experimental.pallas import tpu as pltpu
from jax.sharding import PartitionSpec as P

MESH = pl.DeviceIdType.MESH
F32, BF16 = jnp.float32, jnp.bfloat16
ROWS, COLS = 80, 512
NZ, NY = 16, 4
SUB = 2
WIDTH = COLS // SUB
PIECES = 2 * SUB
STAT = 2 * COLS + 128
PARENT = {1: 0, 2: 1, 3: 2, 4: 0, 5: 4, 6: 5, 7: 6, 8: 7}
ORDER = (1, 4, 2, 5, 3, 6, 7, 8)


def children(s, most):
    return [q for q in range(1, most + 1) if PARENT[q] == s]


def device(xh, xl, y, z, c):
    return (xl * 64 + z * NY + y, xh * 2 + c)


def kernel(total, d_ref, eps_ref, gram_ref, upd_ref,
           q_raw, r_raw, q_c, r_c, z_stat, p_stat, mean, p_out, p_in,
           q_send, q_recv, r_src, r_send, r_recv, zs_send, zs_recv, ps_send, ps_recv, o_send, o_recv):
    s_at, p_at = lax.axis_index("smp"), lax.axis_index("par")
    xl, z, y = s_at // 64, (s_at // NY) % NZ, s_at % NY
    xh, c = p_at // 2, p_at % 2
    other = 1 - c
    half, z_lo = z // 8, z % 8
    me = xl * NY + y
    factor = 1.0 / math.sqrt(total)

    def at_z(step):
        return (z + step + NZ) % NZ

    barrier = pltpu.get_barrier_semaphore()

    def greet(where):
        pl.semaphore_signal(barrier, inc=1, device_id=where, device_id_type=MESH)

    for k in range(1, NZ):
        greet(device(xh, xl, y, at_z(k), c))
    near = [k for k in (1, -1, 4, -4)]
    for k in near:
        greet(device(xh, xl, y, at_z(k), other))
    greet(device(xh, xl, y, z, other))
    for k in range(1, 8):
        g = (me + k) % 8
        for cc in range(2):
            greet(device(xh, g // NY, g % NY, z, cc))
    same = (xl == xh)
    for k in range(8):
        src_xh, src_y = k // NY, k % NY
        is_me = same & (src_xh == xh) & (src_y == y)

        @pl.when(jnp.logical_not(is_me))
        def _():
            greet(device(src_xh, xh, src_y, z, c))

    d = d_ref[...].astype(F32)
    eps = eps_ref[...]
    sums = jnp.sum(d, axis=0, keepdims=True)
    weighted = lax.dot_general(eps, d, (((1,), (0,)), ((), ())), precision=lax.Precision.HIGHEST,
                               preferred_element_type=F32)
    z_stat[z, :, 0:COLS] = sums
    z_stat[z, :, COLS:2 * COLS] = weighted
    z_stat[z, :, 2 * COLS:] = jnp.broadcast_to(jnp.sum(eps, axis=1, keepdims=True), (1, 128))

    pl.semaphore_wait(barrier, 15 + len(near) + 1 + 14 + 8 - same.astype(jnp.int32))

    started = []

    def send(src, dst, s_sem, r_sem, where):
        copy = pltpu.make_async_remote_copy(src_ref=src, dst_ref=dst, send_sem=s_sem, recv_sem=r_sem,
                                            device_id=where, device_id_type=MESH)
        copy.start()
        return copy

    def arrived(ref, sem):
        pltpu.make_async_remote_copy(src_ref=ref, dst_ref=ref, send_sem=sem, recv_sem=sem,
                                     device_id=(s_at, p_at), device_id_type=MESH).wait_recv()

    for k in range(1, NZ):
        started.append(send(z_stat.at[z], z_stat.at[z], zs_send.at[k], zs_recv.at[z],
                            device(xh, xl, y, at_z(k), c)))

    steps = [q for q in (4, 1)]
    targets = [q for q in steps] + [-q for q in steps]
    for i in range(SUB):
        for n, q in enumerate(targets):
            started.append(send(d_ref.at[:, pl.ds(i * WIDTH, WIDTH)], r_raw.at[z_lo, c * SUB + i],
                                r_src.at[n, i], r_recv.at[z_lo, c * SUB + i],
                                device(xh, xl, y, at_z(q), half)))

    def own_copy(i):
        return pltpu.make_async_copy(d_ref.at[:, pl.ds(i * WIDTH, WIDTH)], r_raw.at[z_lo, c * SUB + i],
                                     r_recv.at[z_lo, c * SUB + i])

    def own_send(i):
        return pltpu.make_async_remote_copy(
            src_ref=d_ref.at[:, pl.ds(i * WIDTH, WIDTH)], dst_ref=r_raw.at[z_lo, c * SUB + i],
            send_sem=r_src.at[4, i], recv_sem=r_recv.at[z_lo, c * SUB + i],
            device_id=device(xh, xl, y, z, other), device_id_type=MESH)

    for i in range(SUB):
        @pl.when(half == c)
        def _():
            own_copy(i).start()

        @pl.when(half != c)
        def _():
            own_send(i).start()

    for k in range(1, 8):
        g = (me + k) % 8
        started.append(send(d_ref, q_raw.at[me, c], q_send.at[k], q_recv.at[me, c],
                            device(xh, g // NY, g % NY, z, c)))
    started.append(send(d_ref, q_raw.at[me, c], q_send.at[0], q_recv.at[me, c], device(xh, xl, y, z, other)))

    def pass_on(sign, s, most):
        origin = at_z(-sign * s)

        @pl.when(origin // 8 == c)
        def _():
            lo = origin % 8
            for j in range(PIECES):
                arrived(r_raw.at[lo, j], r_recv.at[lo, j])
                for q in children(s, most):
                    send(r_raw.at[lo, j], r_raw.at[lo, j], r_send.at[lo, j], r_recv.at[lo, j],
                         device(xh, xl, y, at_z(sign * (q - s)), c))

    def pass_both(s):
        pass_on(1, s, 8)
        if s <= 7:
            pass_on(-1, s, 7)

    def forward_plane(k):
        g = (me + k) % 8
        arrived(q_raw.at[g, c], q_recv.at[g, c])
        started.append(send(q_raw.at[g, c], q_raw.at[g, c], q_send.at[8 + k], q_recv.at[g, c],
                            device(xh, xl, y, z, other)))

    pass_both(1)
    pass_both(4)
    pass_both(2)
    pass_both(5)

    for k in range(1, NZ):
        o = at_z(k)
        arrived(z_stat.at[o], zs_recv.at[o])
    total_z = z_stat[0]
    for k in range(1, NZ):
        total_z = total_z + z_stat[k]
    p_stat[me, c] = total_z
    for k in range(1, 8):
        g = (me + k) % 8
        for cc in range(2):
            started.append(send(p_stat.at[me, c], p_stat.at[me, c], ps_send.at[k, cc], ps_recv.at[me, c],
                                device(xh, g // NY, g % NY, z, (c + cc) % 2)))
    started.append(send(p_stat.at[me, c], p_stat.at[me, c], ps_send.at[0, 0], ps_recv.at[me, c],
                        device(xh, xl, y, z, other)))
    pass_both(3)
    for k in range(1, 8):
        forward_plane(k)
    pass_both(6)
    for k in range(8):
        g = (me + k) % 8
        for cc in range(2):
            o = (c + cc) % 2
            if k or cc:
                arrived(p_stat.at[g, o], ps_recv.at[g, o])
    wholes = []
    for o in range(2):
        whole = p_stat[0, o]
        for g in range(1, 8):
            whole = whole + p_stat[g, o]
        wholes.append(whole)
        mean[:, o * COLS:(o + 1) * COLS] = whole[:, 0:COLS] / total
    mine = jnp.where(c == 0, wholes[0], wholes[1])
    upd_ref[...] = (mine[:, COLS:2 * COLS] - (mine[:, 0:COLS] / total) * mine[:, 2 * COLS:2 * COLS + 1]) * factor

    def center(raw, columns):
        return ((raw.astype(F32) - mean[:, columns]) * factor).astype(BF16)

    q_c[pl.ds(me * ROWS, ROWS), pl.ds(pl.multiple_of(c * COLS, COLS), COLS)] = (
        (d_ref[...].astype(F32) - mean[:, pl.ds(pl.multiple_of(c * COLS, COLS), COLS)]) * factor).astype(BF16)
    arrived(q_raw.at[me, other], q_recv.at[me, other])
    q_c[pl.ds(me * ROWS, ROWS), pl.ds(pl.multiple_of(other * COLS, COLS), COLS)] = (
        (q_raw[me, other].astype(F32) - mean[:, pl.ds(pl.multiple_of(other * COLS, COLS), COLS)]) * factor
    ).astype(BF16)
    for k in range(1, 8):
        g = (me + k) % 8
        arrived(q_raw.at[g, other], q_recv.at[g, other])
        for o in range(2):
            q_c[pl.ds(g * ROWS, ROWS), o * COLS:(o + 1) * COLS] = center(q_raw[g, o], slice(o * COLS, (o + 1) * COLS))
    pass_both(7)
    pass_both(8)

    @pl.when(half == c)
    def _():
        for j in range(PIECES):
            arrived(r_raw.at[z_lo, j], r_recv.at[z_lo, j])

    for lo in range(8):
        for j in range(PIECES):
            r_c[lo * ROWS:(lo + 1) * ROWS, j * WIDTH:(j + 1) * WIDTH] = center(
                r_raw[lo, j], slice(j * WIDTH, (j + 1) * WIDTH))

    slot = xh * NY + y

    def product(t):
        part = lax.dot_general(q_c[t * 160:(t + 1) * 160, :], r_c[...], (((1,), (1,)), ((), ())),
                               preferred_element_type=F32).astype(BF16)
        for u in range(2):
            g = 2 * t + u
            p_out[g] = part[u * ROWS:(u + 1) * ROWS]
            is_me = same & (g == me)

            @pl.when(is_me)
            def _():
                pltpu.make_async_copy(p_out.at[g], p_in.at[slot], o_recv.at[slot]).start()

            @pl.when(jnp.logical_not(is_me))
            def _():
                send(p_out.at[g], p_in.at[slot], o_send.at[g], o_recv.at[slot],
                     device(xl, g // NY, g % NY, z, c))

    for t in range(4):
        product(t)

    for k in range(8):
        arrived(p_in.at[k], o_recv.at[k])

    for u in range(5):
        rows = slice(u * 16, (u + 1) * 16)
        added = [p_in[k, rows].astype(F32) + p_in[NY + k, rows].astype(F32) for k in range(NY)]
        for t in range(4):
            gram_ref[rows, t * 640:(t + 1) * 640] = jnp.concatenate(
                [added[k][:, (2 * t + v) * ROWS:(2 * t + v + 1) * ROWS] for v in range(2) for k in range(NY)], axis=1)

    for copy in started:
        copy.wait_send()
    for i in range(SUB):
        @pl.when(half != c)
        def _():
            own_send(i).wait_send()
    for sign, most in ((1, 8), (-1, 7)):
        for s in range(1, most):
            origin = at_z(-sign * s)
            if children(s, most):
                @pl.when(origin // 8 == c)
                def _():
                    lo = origin % 8
                    for j in range(PIECES):
                        pltpu.make_async_remote_copy(
                            src_ref=r_raw.at[lo, j], dst_ref=r_raw.at[lo, j], send_sem=r_send.at[lo, j],
                            recv_sem=r_recv.at[lo, j], device_id=(s_at, p_at), device_id_type=MESH).wait_send()
    for g in range(8):
        @pl.when(jnp.logical_not(same & (g == me)))
        def _():
            pltpu.make_async_remote_copy(
                src_ref=p_out.at[g], dst_ref=p_in.at[slot], send_sem=o_send.at[g], recv_sem=o_recv.at[slot],
                device_id=(s_at, p_at), device_id_type=MESH).wait_send()


def shards(derivatives, epsilon):
    total = derivatives.shape[0] * 128
    dma = pltpu.SemaphoreType.DMA
    gram, upd = pl.pallas_call(
        functools.partial(kernel, total),
        name="gram",
        out_shape=(jax.ShapeDtypeStruct((ROWS, 2560), F32), jax.ShapeDtypeStruct((1, COLS), F32)),
        in_specs=[pl.BlockSpec(memory_space=pltpu.VMEM)] * 2,
        out_specs=[pl.BlockSpec(memory_space=pltpu.VMEM)] * 2,
        scratch_shapes=[
            pltpu.VMEM((8, 2, ROWS, COLS), BF16),
            pltpu.VMEM((8, PIECES, ROWS, WIDTH), BF16),
            pltpu.VMEM((640, 2 * COLS), BF16),
            pltpu.VMEM((640, 2 * COLS), BF16),
            pltpu.VMEM((NZ, 1, STAT), F32),
            pltpu.VMEM((8, 2, 1, STAT), F32),
            pltpu.VMEM((1, 2 * COLS), F32),
            pltpu.VMEM((8, ROWS, 640), BF16),
            pltpu.VMEM((8, ROWS, 640), BF16),
            dma((16,)), dma((8, 2)),
            dma((5, SUB)), dma((8, PIECES)), dma((8, PIECES)),
            dma((NZ,)), dma((NZ,)),
            dma((8, 2)), dma((8, 2)),
            dma((8,)), dma((8,)),
        ],
        compiler_params=pltpu.CompilerParams(collective_id=0, has_side_effects=True, vmem_limit_bytes=48 << 20),
    )(derivatives, epsilon.reshape(1, ROWS))
    return gram, upd.reshape(COLS)


def solution(mesh):
    in_specs = (P("smp", "par"), P("smp"))
    out_specs = (P("smp", "par"), P("par"))
    return jax.shard_map(shards, mesh=mesh, in_specs=in_specs, out_specs=out_specs, check_vma=False)
```

time: 1250 us -> 68 us (0.05)
  the two profiles are of different devices: /device:TPU:24 before, /device:TPU:27 now
where the time goes in v1:
time: 68 us; the launch traced here: 67.8 us
  Pallas kernels  64.1 us (94%)
  local copies, waits for them, and re-layouts  3.01 us (4%)
    pallas_call x1, Pallas kernels, shards(): pl.pallas_call(functools.partial(kernel, total), name='gram', out_shape=(...  64.1 us
    unnamed x6, local copies, waits for them, and re-layouts  3.01 us

profile of v1, /device:TPU:27, one launch (start us, length us, event | category | flops | bytes accessed | tf_op | source)
XLA Modules:
  0.0 67.8 jit_solution(18079403094611428139)
XLA Ops:
  0.6 0.0 copy-start.1
  0.6 0.6 copy-done.1
  1.3 0.0 copy-start
  1.3 0.9 %copy-done = bf16[80,512]{1,0:T(8,128)(2,1)S(1)} copy-done((bf16[80,512]{1,0:T(8,128)(2,1)S(1)}, bf16[80,512]{1,0:T(8,128)(2,1)}, u32[]{:S(2)}) %copy-start) | copy-done | bytes 81944
  2.2 64.1 %gram.1 = (f32[80,2560]{1,0:T(8,128)S(1)}, f32[1,512]{1,0:T(1,128)S(1)}) custom-call(bf16[80,512]{1,0:T(8,128)(2,1)S(1)} %copy-done, f32[1,80]{1,0:T(1,128)S(1)} %bitcast.3), custom_call_target="tpu_custom_call" | custom-call | tf_op jit(solution)/shard_map/gram/pallas_call | solution.py:278
  66.3 0.9 %copy.6 = f32[80,2560]{1,0:T(8,128)} copy(f32[80,2560]{1,0:T(8,128)S(1)} %get-tuple-element.8) | data formatting | bytes 1638400
  67.2 0.6 copy.7
Async XLA Ops:
  0.6 0.7 copy-start.1
  1.3 0.9 %copy-start = (bf16[80,512]{1,0:T(8,128)(2,1)S(1)}, bf16[80,512]{1,0:T(8,128)(2,1)}, u32[]{:S(2)}) copy-start(bf16[80,512]{1,0:T(8,128)(2,1)} %d_ref.1) | copy-start | bytes 245764

commit v2 on v1

v2 whole, which is shorter than its diff:
```python
import functools
import math

import jax
import jax.numpy as jnp
from jax import lax
from jax.experimental import pallas as pl
from jax.experimental.pallas import tpu as pltpu
from jax.sharding import PartitionSpec as P

MESH = pl.DeviceIdType.MESH
F32, BF16 = jnp.float32, jnp.bfloat16
ROWS, COLS = 80, 512
NZ, NY = 16, 4
SUB = 2
WIDTH = COLS // SUB
PIECES = 2 * SUB
GROUP = 4 * ROWS
STAT = 2 * COLS + 128
NEAR = (1, -1, 2, -2, 3, -3)
FAR = 6
LOOP_FROM = 5


def device(xh, xl, y, z, c):
    return (xl * 64 + z * NY + y, xh * 2 + c)


def kernel(total, d_hbm, eps_ref, gram_ref, upd_ref,
           d_ref, q_raw, r_raw, q_c, r_c, stat, z_near, z_out, z_far, p_stat, mean, p_out, p_in,
           d_sem, q_send, q_recv, r_src, r_send, r_recv, zn_send, zn_recv, zf_send, zf_recv,
           ps_send, ps_recv, o_send, o_recv):
    s_at, p_at = lax.axis_index("smp"), lax.axis_index("par")
    xl, z, y = s_at // 64, (s_at // NY) % NZ, s_at % NY
    xh, c = p_at // 2, p_at % 2
    other = 1 - c
    half, z_lo = z // 8, z % 8
    me = xl * NY + y
    factor = 1.0 / math.sqrt(total)
    load = pltpu.make_async_copy(d_hbm, d_ref, d_sem)
    load.start()

    def at_z(step):
        return (z + step + NZ) % NZ

    barrier = pltpu.get_barrier_semaphore()

    def greet(where):
        pl.semaphore_signal(barrier, inc=1, device_id=where, device_id_type=MESH)

    same = (xl == xh)
    for k in range(8):
        src_xh, src_y = k // NY, k % NY

        @pl.when(jnp.logical_not(same & (src_xh == xh) & (src_y == y)))
        def _():
            greet(device(src_xh, xh, src_y, z, c))

    for k in NEAR:
        greet(device(xh, xl, y, at_z(k), c))
    for k in (1, -1):
        greet(device(xh, xl, y, at_z(k), other))
    for k in range(1, 8):
        g = (me + k) % 8
        for cc in range(2):
            greet(device(xh, g // NY, g % NY, z, cc))
    greet(device(xh, xl, y, z, other))

    load.wait()
    d = d_ref[...].astype(F32)
    eps = eps_ref[...]
    stat[:, 0:COLS] = jnp.sum(d, axis=0, keepdims=True)
    stat[:, COLS:2 * COLS] = lax.dot_general(
        eps, d, (((1,), (0,)), ((), ())), precision=lax.Precision.HIGHEST, preferred_element_type=F32)
    stat[:, 2 * COLS:] = jnp.broadcast_to(jnp.sum(eps, axis=1, keepdims=True), (1, 128))

    pl.semaphore_wait(barrier, 8 - same.astype(jnp.int32) + len(NEAR) + 2 + 14 + 1)

    started = []

    def send(src, dst, s_sem, r_sem, where):
        copy = pltpu.make_async_remote_copy(src_ref=src, dst_ref=dst, send_sem=s_sem, recv_sem=r_sem,
                                            device_id=where, device_id_type=MESH)
        copy.start()
        return copy

    def handle(ref, sem):
        return pltpu.make_async_remote_copy(src_ref=ref, dst_ref=ref, send_sem=sem, recv_sem=sem,
                                            device_id=(s_at, p_at), device_id_type=MESH)

    def arrived(ref, sem):
        handle(ref, sem).wait_recv()

    for n, k in enumerate(NEAR):
        started.append(send(stat, z_near.at[n], zn_send.at[n], zn_recv.at[n], device(xh, xl, y, at_z(-k), c)))

    for i in range(SUB):
        for n, q in enumerate((1, -1)):
            started.append(send(d_ref.at[:, pl.ds(i * WIDTH, WIDTH)], r_raw.at[z_lo, c * SUB + i],
                                r_src.at[n, i], r_recv.at[z_lo, c * SUB + i],
                                device(xh, xl, y, at_z(q), half)))

    def own_copy(i):
        return pltpu.make_async_copy(d_ref.at[:, pl.ds(i * WIDTH, WIDTH)], r_raw.at[z_lo, c * SUB + i],
                                     r_recv.at[z_lo, c * SUB + i])

    def own_send(i):
        return pltpu.make_async_remote_copy(
            src_ref=d_ref.at[:, pl.ds(i * WIDTH, WIDTH)], dst_ref=r_raw.at[z_lo, c * SUB + i],
            send_sem=r_src.at[2, i], recv_sem=r_recv.at[z_lo, c * SUB + i],
            device_id=device(xh, xl, y, z, other), device_id_type=MESH)

    for i in range(SUB):
        @pl.when(half == c)
        def _():
            own_copy(i).start()

        @pl.when(half != c)
        def _():
            own_send(i).start()

    for k in range(1, 8):
        g = (me + k) % 8
        started.append(send(d_ref, q_raw.at[me, c], q_send.at[k], q_recv.at[me, c],
                            device(xh, g // NY, g % NY, z, c)))
    started.append(send(d_ref, q_raw.at[me, c], q_send.at[0], q_recv.at[me, c], device(xh, xl, y, z, other)))

    def pass_on(sign, s, most):
        origin = at_z(-sign * s)
        lo = origin % 8

        @pl.when((origin // 8 == c) & (s < most))
        def _():
            for j in range(PIECES):
                arrived(r_raw.at[lo, j], r_recv.at[lo, j])
                send(r_raw.at[lo, j], r_raw.at[lo, j], r_send.at[lo, j], r_recv.at[lo, j],
                     device(xh, xl, y, at_z(sign), c))

        @pl.when((origin // 8 == c) & (s == most))
        def _():
            for j in range(PIECES):
                arrived(r_raw.at[lo, j], r_recv.at[lo, j])

    def pass_both(s):
        pass_on(1, s, 8)
        pass_on(-1, s, 7)

    pass_both(1)

    for n in range(len(NEAR)):
        arrived(z_near.at[n], zn_recv.at[n])
    up = {k: n for n, k in enumerate(NEAR)}

    def gathered(ks):
        whole = stat[...]
        for k in ks:
            whole = whole + z_near[up[k]]
        return whole

    z_out[0] = gathered((-1, 1, 2))
    z_out[1] = gathered((-2, -1, 1, 2))
    for n, k in enumerate((FAR, -FAR)):
        started.append(send(z_out.at[n], z_far.at[n], zf_send.at[n], zf_recv.at[n], device(xh, xl, y, at_z(k), c)))

    pass_both(2)
    pass_both(3)
    for n in range(2):
        arrived(z_far.at[n], zf_recv.at[n])
    p_stat[me, c] = gathered(NEAR) + z_far[0] + z_far[1]

    for k in range(1, 8):
        g = (me + k) % 8
        for cc in range(2):
            started.append(send(p_stat.at[me, c], p_stat.at[me, c], ps_send.at[k, cc], ps_recv.at[me, c],
                                device(xh, g // NY, g % NY, z, (c + cc) % 2)))
    started.append(send(p_stat.at[me, c], p_stat.at[me, c], ps_send.at[0, 0], ps_recv.at[me, c],
                        device(xh, xl, y, z, other)))
    for k in range(1, 8):
        g = (me + k) % 8
        arrived(q_raw.at[g, c], q_recv.at[g, c])
        started.append(send(q_raw.at[g, c], q_raw.at[g, c], q_send.at[8 + k], q_recv.at[g, c],
                            device(xh, xl, y, z, other)))
    pass_both(4)
    pass_both(5)
    for k in range(8):
        g = (me + k) % 8
        for cc in range(2):
            o = (c + cc) % 2
            if k or cc:
                arrived(p_stat.at[g, o], ps_recv.at[g, o])
    wholes = []
    for o in range(2):
        whole = p_stat[0, o]
        for g in range(1, 8):
            whole = whole + p_stat[g, o]
        wholes.append(whole)
        mean[:, o * COLS:(o + 1) * COLS] = whole[:, 0:COLS] / total
    mine = jnp.where(c == 0, wholes[0], wholes[1])
    upd_ref[...] = (mine[:, COLS:2 * COLS] - (mine[:, 0:COLS] / total) * mine[:, 2 * COLS:2 * COLS + 1]) * factor

    def center(raw, columns):
        return ((raw.astype(F32) - mean[:, columns]) * factor).astype(BF16)

    here, there = (pl.ds(pl.multiple_of(o * COLS, COLS), COLS) for o in (c, other))
    q_c[pl.ds(me * ROWS, ROWS), here] = center(d_ref[...], here)
    arrived(q_raw.at[me, other], q_recv.at[me, other])
    q_c[pl.ds(me * ROWS, ROWS), there] = center(q_raw[me, other], there)
    for k in range(1, 8):
        g = (me + k) % 8
        arrived(q_raw.at[g, other], q_recv.at[g, other])
        for o in range(2):
            q_c[pl.ds(g * ROWS, ROWS), o * COLS:(o + 1) * COLS] = center(q_raw[g, o], slice(o * COLS, (o + 1) * COLS))

    @pl.when(half == c)
    def _():
        for j in range(PIECES):
            arrived(r_raw.at[z_lo, j], r_recv.at[z_lo, j])

    slot = xh * NY + y

    def out_is_me(g):
        return same & (g == me)

    def group_at(t):
        most = LOOP_FROM
        for v in range(4):
            up_steps = (z - (c * 8 + t * 4 + v) + NZ) % NZ
            most = jnp.maximum(most, jnp.minimum(up_steps, NZ - up_steps))
        return most

    def product(t):
        for v in range(4):
            for j in range(PIECES):
                r_c[v * ROWS:(v + 1) * ROWS, j * WIDTH:(j + 1) * WIDTH] = center(
                    r_raw[t * 4 + v, j], slice(j * WIDTH, (j + 1) * WIDTH))
        for u in range(4):
            part = lax.dot_general(q_c[u * 160:(u + 1) * 160, :], r_c[...], (((1,), (1,)), ((), ())),
                                   preferred_element_type=F32).astype(BF16)
            for g in (2 * u, 2 * u + 1):
                p_out[t, g] = part[(g - 2 * u) * ROWS:(g - 2 * u + 1) * ROWS]

                @pl.when(out_is_me(g))
                def _():
                    pltpu.make_async_copy(p_out.at[t, g], p_in.at[t, slot], o_recv.at[t, slot]).start()

                @pl.when(jnp.logical_not(out_is_me(g)))
                def _():
                    send(p_out.at[t, g], p_in.at[t, slot], o_send.at[t, g], o_recv.at[t, slot],
                         device(xl, g // NY, g % NY, z, c))

    def step(s, carry):
        @pl.when(s > LOOP_FROM)
        def _():
            pass_both(s)

        def one(t, inner):
            @pl.when(group_at(t) == s)
            def _():
                product(t)
            return inner

        return lax.fori_loop(0, 2, one, carry)

    lax.fori_loop(LOOP_FROM, 9, step, 0)

    first = (group_at(1) < group_at(0)).astype(jnp.int32)

    def assemble(n, carry):
        t = jnp.where(n == 0, first, 1 - first)
        for k in range(8):
            arrived(p_in.at[t, k], o_recv.at[t, k])
        for u in range(5):
            rows = slice(u * 16, (u + 1) * 16)
            added = [p_in[t, k, rows].astype(F32) + p_in[t, NY + k, rows].astype(F32) for k in range(NY)]
            for w in range(2):
                gram_ref[rows, pl.ds(pl.multiple_of(t * 1280 + w * 640, 640), 640)] = jnp.concatenate(
                    [added[k][:, (2 * w + v) * ROWS:(2 * w + v + 1) * ROWS] for v in range(2) for k in range(NY)],
                    axis=1)
        return carry

    lax.fori_loop(0, 2, assemble, 0)

    for copy in started:
        copy.wait_send()
    for i in range(SUB):
        @pl.when(half != c)
        def _():
            own_send(i).wait_send()
    for sign, most in ((1, 8), (-1, 7)):
        for s in range(1, most):
            origin = at_z(-sign * s)

            @pl.when(origin // 8 == c)
            def _():
                for j in range(PIECES):
                    handle(r_raw.at[origin % 8, j], r_send.at[origin % 8, j]).wait_send()
    for t in range(2):
        for g in range(8):
            @pl.when(jnp.logical_not(out_is_me(g)))
            def _():
                handle(p_out.at[t, g], o_send.at[t, g]).wait_send()


def shards(derivatives, epsilon):
    total = derivatives.shape[0] * 128
    dma = pltpu.SemaphoreType.DMA
    gram, upd = pl.pallas_call(
        functools.partial(kernel, total),
        name="gram",
        out_shape=(jax.ShapeDtypeStruct((ROWS, 2560), F32), jax.ShapeDtypeStruct((1, COLS), F32)),
        in_specs=[pl.BlockSpec(memory_space=pl.ANY), pl.BlockSpec(memory_space=pltpu.VMEM)],
        out_specs=[pl.BlockSpec(memory_space=pltpu.VMEM)] * 2,
        scratch_shapes=[
            pltpu.VMEM((ROWS, COLS), BF16),
            pltpu.VMEM((8, 2, ROWS, COLS), BF16),
            pltpu.VMEM((8, PIECES, ROWS, WIDTH), BF16),
            pltpu.VMEM((640, 2 * COLS), BF16),
            pltpu.VMEM((GROUP, 2 * COLS), BF16),
            pltpu.VMEM((1, STAT), F32),
            pltpu.VMEM((len(NEAR), 1, STAT), F32),
            pltpu.VMEM((2, 1, STAT), F32),
            pltpu.VMEM((2, 1, STAT), F32),
            pltpu.VMEM((8, 2, 1, STAT), F32),
            pltpu.VMEM((1, 2 * COLS), F32),
            pltpu.VMEM((2, 8, ROWS, GROUP), BF16),
            pltpu.VMEM((2, 8, ROWS, GROUP), BF16),
            dma,
            dma((16,)), dma((8, 2)),
            dma((3, SUB)), dma((8, PIECES)), dma((8, PIECES)),
            dma((len(NEAR),)), dma((len(NEAR),)), dma((2,)), dma((2,)),
            dma((8, 2)), dma((8, 2)),
            dma((2, 8)), dma((2, 8)),
        ],
        compiler_params=pltpu.CompilerParams(collective_id=0, has_side_effects=True, vmem_limit_bytes=24 << 20),
    )(derivatives, epsilon.reshape(1, ROWS))
    return gram, upd.reshape(COLS)


def solution(mesh):
    in_specs = (P("smp", "par"), P("smp"))
    out_specs = (P("smp", "par"), P("par"))
    return jax.shard_map(shards, mesh=mesh, in_specs=in_specs, out_specs=out_specs, check_vma=False)
```

time: 68 us -> 55 us (0.81)
  Pallas kernels: 64.1 us -> 51.2 us
    pallas_call x1, Pallas kernels: 64.1 us -> 51.2 us  [shards(): pl.pallas_call(functools.partial(kernel, total), name='gram', out_shape=(...]
where the time goes in v2:
time: 55 us; the launch traced here: 54.9 us
  Pallas kernels  51.2 us (93%)
  local copies, waits for them, and re-layouts  3.01 us (5%)
  between operations  0.65 us (1%)
    pallas_call x1, Pallas kernels, shards(): pl.pallas_call(functools.partial(kernel, total), name='gram', out_shape=(...  51.2 us
    unnamed x6, local copies, waits for them, and re-layouts  3.01 us

profile of v2, /device:TPU:27, one launch (start us, length us, event | category | flops | bytes accessed | tf_op | source)
XLA Modules:
  0.0 54.9 jit_solution(5172428286485829895)
XLA Ops:
  0.6 0.0 copy-start.1
  0.6 0.6 %copy-done.1 = f32[80]{0:T(128)S(1)} copy-done((f32[80]{0:T(128)S(1)}, f32[80]{0:T(128)}, u32[]{:S(2)}) %copy-start.1) | copy-done | bytes 344
  1.3 0.0 copy-start
  1.3 0.9 %copy-done = bf16[80,512]{1,0:T(8,128)(2,1)S(1)} copy-done((bf16[80,512]{1,0:T(8,128)(2,1)S(1)}, bf16[80,512]{1,0:T(8,128)(2,1)}, u32[]{:S(2)}) %copy-start) | copy-done | bytes 81944
  2.2 51.2 %gram.1 = (f32[80,2560]{1,0:T(8,128)S(1)}, f32[1,512]{1,0:T(1,128)S(1)}) custom-call(bf16[80,512]{1,0:T(8,128)(2,1)S(1)} %copy-done, f32[1,80]{1,0:T(1,128)S(1)} %bitcast.3), custom_call_target="tpu_custom_call" | custom-call | tf_op jit(solution)/shard_map/gram/pallas_call | solution.py:307
  53.4 0.9 %copy.6 = f32[80,2560]{1,0:T(8,128)} copy(f32[80,2560]{1,0:T(8,128)S(1)} %get-tuple-element.8) | data formatting | bytes 1638400
  54.3 0.6 %copy.7 = f32[512]{0:T(512)} copy(f32[512]{0:T(512)S(1)} %bitcast.2) | data formatting | bytes 4096
Async XLA Ops:
  0.6 0.7 %copy-start.1 = (f32[80]{0:T(128)S(1)}, f32[80]{0:T(128)}, u32[]{:S(2)}) copy-start(f32[80]{0:T(128)} %param.3) | copy-start | bytes 964
  1.3 0.9 %copy-start = (bf16[80,512]{1,0:T(8,128)(2,1)S(1)}, bf16[80,512]{1,0:T(8,128)(2,1)}, u32[]{:S(2)}) copy-start(bf16[80,512]{1,0:T(8,128)(2,1)} %d_hbm.1) | copy-start | bytes 245764

commit v3 on v2

--- a/solution.py
+++ b/solution.py
@@ -15,7 +15,7 @@
 SUB = 2
 WIDTH = COLS // SUB
 PIECES = 2 * SUB
-GROUP = 4 * ROWS
+SPLIT = 256
 STAT = 2 * COLS + 128
 NEAR = (1, -1, 2, -2, 3, -3)
 FAR = 6
@@ -27,8 +27,8 @@
 
 
 def kernel(total, d_hbm, eps_ref, gram_ref, upd_ref,
-           d_ref, q_raw, r_raw, q_c, r_c, stat, z_near, z_out, z_far, p_stat, mean, p_out, p_in,
-           d_sem, q_send, q_recv, r_src, r_send, r_recv, zn_send, zn_recv, zf_send, zf_recv,
+           d_ref, q_raw, r_raw, q_c, r_c, stat, z_near, z_out, z_far, p_stat, mean, p_out0, p_out1, p_in0, p_in1,
+           d_sem, q_own, q_send, q_recv, r_src, r_send, r_recv, zn_send, zn_recv, zf_send, zf_recv,
            ps_send, ps_recv, o_send, o_recv):
     s_at, p_at = lax.axis_index("smp"), lax.axis_index("par")
     xl, z, y = s_at // 64, (s_at // NY) % NZ, s_at % NY
@@ -118,6 +118,9 @@
         @pl.when(half != c)
         def _():
             own_send(i).start()
+
+    own_here = pltpu.make_async_copy(d_ref, q_raw.at[me, c], q_own)
+    own_here.start()
 
     for k in range(1, 8):
         g = (me + k) % 8
@@ -201,15 +204,19 @@
     def center(raw, columns):
         return ((raw.astype(F32) - mean[:, columns]) * factor).astype(BF16)
 
-    here, there = (pl.ds(pl.multiple_of(o * COLS, COLS), COLS) for o in (c, other))
-    q_c[pl.ds(me * ROWS, ROWS), here] = center(d_ref[...], here)
-    arrived(q_raw.at[me, other], q_recv.at[me, other])
-    q_c[pl.ds(me * ROWS, ROWS), there] = center(q_raw[me, other], there)
-    for k in range(1, 8):
-        g = (me + k) % 8
-        arrived(q_raw.at[g, other], q_recv.at[g, other])
-        for o in range(2):
-            q_c[pl.ds(g * ROWS, ROWS), o * COLS:(o + 1) * COLS] = center(q_raw[g, o], slice(o * COLS, (o + 1) * COLS))
+    for k in range(8):
+        g = (me + k) % 8
+        if k:
+            arrived(q_raw.at[g, other], q_recv.at[g, other])
+        else:
+            own_here.wait()
+            arrived(q_raw.at[me, other], q_recv.at[me, other])
+
+    def center_pair(u):
+        for v in range(2):
+            for o in range(2):
+                q_c[pl.ds(u * 160 + v * ROWS, ROWS), o * COLS:(o + 1) * COLS] = center(
+                    q_raw[2 * u + v, o], slice(o * COLS, (o + 1) * COLS))
 
     @pl.when(half == c)
     def _():
@@ -217,35 +224,54 @@
             arrived(r_raw.at[z_lo, j], r_recv.at[z_lo, j])
 
     slot = xh * NY + y
+    outs = ((p_out0, p_in0, slice(0, SPLIT), range(4)), (p_out1, p_in1, slice(SPLIT, 640), range(3, 8)))
 
     def out_is_me(g):
         return same & (g == me)
 
-    def group_at(t):
+    def ready_at(los):
         most = LOOP_FROM
-        for v in range(4):
-            up_steps = (z - (c * 8 + t * 4 + v) + NZ) % NZ
+        for v in los:
+            up_steps = (z - (c * 8 + v) + NZ) % NZ
             most = jnp.maximum(most, jnp.minimum(up_steps, NZ - up_steps))
         return most
 
+    ready = [ready_at(outs[t][3]) for t in range(2)]
+    early = jnp.minimum(ready[0], ready[1]) == LOOP_FROM
+    leads = (ready[0] <= ready[1], ready[1] < ready[0])
+    turn = y + 2 * xh
+
+    @pl.when(jnp.logical_not(early))
+    def _():
+        for u in range(4):
+            center_pair(u)
+
     def product(t):
-        for v in range(4):
+        p_out, p_in, columns, los = outs[t]
+        for v in los:
             for j in range(PIECES):
                 r_c[v * ROWS:(v + 1) * ROWS, j * WIDTH:(j + 1) * WIDTH] = center(
-                    r_raw[t * 4 + v, j], slice(j * WIDTH, (j + 1) * WIDTH))
-        for u in range(4):
-            part = lax.dot_general(q_c[u * 160:(u + 1) * 160, :], r_c[...], (((1,), (1,)), ((), ())),
+                    r_raw[v, j], slice(j * WIDTH, (j + 1) * WIDTH))
+        for i in range(4):
+            u = (turn + i) % 4
+
+            @pl.when(early & leads[t])
+            def _():
+                center_pair(u)
+
+            part = lax.dot_general(q_c[pl.ds(u * 160, 160), :], r_c[columns, :], (((1,), (1,)), ((), ())),
                                    preferred_element_type=F32).astype(BF16)
-            for g in (2 * u, 2 * u + 1):
-                p_out[t, g] = part[(g - 2 * u) * ROWS:(g - 2 * u + 1) * ROWS]
+            for v in range(2):
+                g = 2 * u + v
+                p_out[g] = part[v * ROWS:(v + 1) * ROWS]
 
                 @pl.when(out_is_me(g))
                 def _():
-                    pltpu.make_async_copy(p_out.at[t, g], p_in.at[t, slot], o_recv.at[t, slot]).start()
+                    pltpu.make_async_copy(p_out.at[g], p_in.at[slot], o_recv.at[t, slot]).start()
 
                 @pl.when(jnp.logical_not(out_is_me(g)))
                 def _():
-                    send(p_out.at[t, g], p_in.at[t, slot], o_send.at[t, g], o_recv.at[t, slot],
+                    send(p_out.at[g], p_in.at[slot], o_send.at[t, g], o_recv.at[t, slot],
                          device(xl, g // NY, g % NY, z, c))
 
     def step(s, carry):
@@ -253,32 +279,13 @@
         def _():
             pass_both(s)
 
-        def one(t, inner):
-            @pl.when(group_at(t) == s)
+        for t in range(2):
+            @pl.when(ready[t] == s)
             def _():
                 product(t)
-            return inner
-
-        return lax.fori_loop(0, 2, one, carry)
+        return carry
 
     lax.fori_loop(LOOP_FROM, 9, step, 0)
-
-    first = (group_at(1) < group_at(0)).astype(jnp.int32)
-
-    def assemble(n, carry):
-        t = jnp.where(n == 0, first, 1 - first)
-        for k in range(8):
-            arrived(p_in.at[t, k], o_recv.at[t, k])
-        for u in range(5):
-            rows = slice(u * 16, (u + 1) * 16)
-            added = [p_in[t, k, rows].astype(F32) + p_in[t, NY + k, rows].astype(F32) for k in range(NY)]
-            for w in range(2):
-                gram_ref[rows, pl.ds(pl.multiple_of(t * 1280 + w * 640, 640), 640)] = jnp.concatenate(
-                    [added[k][:, (2 * w + v) * ROWS:(2 * w + v + 1) * ROWS] for v in range(2) for k in range(NY)],
-                    axis=1)
-        return carry
-
-    lax.fori_loop(0, 2, assemble, 0)
 
     for copy in started:
         copy.wait_send()
@@ -298,7 +305,18 @@
         for g in range(8):
             @pl.when(jnp.logical_not(out_is_me(g)))
             def _():
-                handle(p_out.at[t, g], o_send.at[t, g]).wait_send()
+                handle(outs[t][0].at[g], o_send.at[t, g]).wait_send()
+
+    for t in range(2):
+        for k in range(8):
+            arrived(outs[t][1].at[k], o_recv.at[t, k])
+    for u in range(5):
+        rows = slice(u * 16, (u + 1) * 16)
+        added = [jnp.concatenate([p_in[k, rows].astype(F32) + p_in[NY + k, rows].astype(F32)
+                                  for p_in in (p_in0, p_in1)], axis=1) for k in range(NY)]
+        for w in range(4):
+            gram_ref[rows, w * 640:(w + 1) * 640] = jnp.concatenate(
+                [added[k][:, (2 * w + v) * ROWS:(2 * w + v + 1) * ROWS] for v in range(2) for k in range(NY)], axis=1)
 
 
 def shards(derivatives, epsilon):
@@ -315,16 +333,18 @@
             pltpu.VMEM((8, 2, ROWS, COLS), BF16),
             pltpu.VMEM((8, PIECES, ROWS, WIDTH), BF16),
             pltpu.VMEM((640, 2 * COLS), BF16),
-            pltpu.VMEM((GROUP, 2 * COLS), BF16),
+            pltpu.VMEM((640, 2 * COLS), BF16),
             pltpu.VMEM((1, STAT), F32),
             pltpu.VMEM((len(NEAR), 1, STAT), F32),
             pltpu.VMEM((2, 1, STAT), F32),
             pltpu.VMEM((2, 1, STAT), F32),
             pltpu.VMEM((8, 2, 1, STAT), F32),
             pltpu.VMEM((1, 2 * COLS), F32),
-            pltpu.VMEM((2, 8, ROWS, GROUP), BF16),
-            pltpu.VMEM((2, 8, ROWS, GROUP), BF16),
-            dma,
+            pltpu.VMEM((8, ROWS, SPLIT), BF16),
+            pltpu.VMEM((8, ROWS, 640 - SPLIT), BF16),
+            pltpu.VMEM((8, ROWS, SPLIT), BF16),
+            pltpu.VMEM((8, ROWS, 640 - SPLIT), BF16),
+            dma, dma,
             dma((16,)), dma((8, 2)),
             dma((3, SUB)), dma((8, PIECES)), dma((8, PIECES)),
             dma((len(NEAR),)), dma((len(NEAR),)), dma((2,)), dma((2,)),

time: 55 us -> 54.3 us (0.987)
  the two profiles are of different devices: /device:TPU:27 before, /device:TPU:24 now
where the time goes in v3:
time: 54.3 us; the launch traced here: 54.1 us
  Pallas kernels  50.4 us (93%)
  local copies, waits for them, and re-layouts  3.01 us (6%)
  between operations  0.65 us (1%)
    pallas_call x1, Pallas kernels, shards(): pl.pallas_call(functools.partial(kernel, total), name='gram', out_shape=(...  50.4 us
    unnamed x6, local copies, waits for them, and re-layouts  3.01 us

profile of v3, /device:TPU:24, one launch (start us, length us, event | category | flops | bytes accessed | tf_op | source)
XLA Modules:
  0.0 54.1 jit_solution(16723560900587442810)
XLA Ops:
  0.6 0.0 copy-start.1
  0.6 0.6 %copy-done.1 = f32[80]{0:T(128)S(1)} copy-done((f32[80]{0:T(128)S(1)}, f32[80]{0:T(128)}, u32[]{:S(2)}) %copy-start.1) | copy-done | bytes 344
  1.3 0.0 copy-start
  1.3 0.9 %copy-done = bf16[80,512]{1,0:T(8,128)(2,1)S(1)} copy-done((bf16[80,512]{1,0:T(8,128)(2,1)S(1)}, bf16[80,512]{1,0:T(8,128)(2,1)}, u32[]{:S(2)}) %copy-start) | copy-done | bytes 81944
  2.2 50.4 %gram.1 = (f32[80,2560]{1,0:T(8,128)S(1)}, f32[1,512]{1,0:T(1,128)S(1)}) custom-call(bf16[80,512]{1,0:T(8,128)(2,1)S(1)} %copy-done, f32[1,80]{1,0:T(1,128)S(1)} %bitcast.3), custom_call_target="tpu_custom_call" | custom-call | tf_op jit(solution)/shard_map/gram/pallas_call | solution.py:325
  52.6 0.9 %copy.6 = f32[80,2560]{1,0:T(8,128)} copy(f32[80,2560]{1,0:T(8,128)S(1)} %get-tuple-element.8) | data formatting | bytes 1638400
  53.5 0.6 %copy.7 = f32[512]{0:T(512)} copy(f32[512]{0:T(512)S(1)} %bitcast.2) | data formatting | bytes 4096
Async XLA Ops:
  0.6 0.7 %copy-start.1 = (f32[80]{0:T(128)S(1)}, f32[80]{0:T(128)}, u32[]{:S(2)}) copy-start(f32[80]{0:T(128)} %param.3) | copy-start | bytes 964
  1.3 0.9 %copy-start = (bf16[80,512]{1,0:T(8,128)(2,1)S(1)}, bf16[80,512]{1,0:T(8,128)(2,1)}, u32[]{:S(2)}) copy-start(bf16[80,512]{1,0:T(8,128)(2,1)} %d_hbm.1) | copy-start | bytes 245764

commit v4 on v3

--- a/solution.py
+++ b/solution.py
@@ -12,7 +12,7 @@
 F32, BF16 = jnp.float32, jnp.bfloat16
 ROWS, COLS = 80, 512
 NZ, NY = 16, 4
-SUB = 2
+SUB = 4
 WIDTH = COLS // SUB
 PIECES = 2 * SUB
 SPLIT = 256
@@ -20,14 +20,15 @@
 NEAR = (1, -1, 2, -2, 3, -3)
 FAR = 6
 LOOP_FROM = 5
+ASSEMBLE_VMEM = 16 << 20
 
 
 def device(xh, xl, y, z, c):
     return (xl * 64 + z * NY + y, xh * 2 + c)
 
 
-def kernel(total, d_hbm, eps_ref, gram_ref, upd_ref,
-           d_ref, q_raw, r_raw, q_c, r_c, stat, z_near, z_out, z_far, p_stat, mean, p_out0, p_out1, p_in0, p_in1,
+def kernel(total, d_hbm, eps_ref, p_in0, p_in1, upd_ref,
+           d_ref, q_raw, r_raw, q_c, r_c, stat, z_near, z_out, z_far, p_stat, mean, p_out0, p_out1,
            d_sem, q_own, q_send, q_recv, r_src, r_send, r_recv, zn_send, zn_recv, zf_send, zf_recv,
            ps_send, ps_recv, o_send, o_recv):
     s_at, p_at = lax.axis_index("smp"), lax.axis_index("par")
@@ -128,25 +129,20 @@
                             device(xh, g // NY, g % NY, z, c)))
     started.append(send(d_ref, q_raw.at[me, c], q_send.at[0], q_recv.at[me, c], device(xh, xl, y, z, other)))
 
-    def pass_on(sign, s, most):
-        origin = at_z(-sign * s)
-        lo = origin % 8
-
-        @pl.when((origin // 8 == c) & (s < most))
-        def _():
-            for j in range(PIECES):
-                arrived(r_raw.at[lo, j], r_recv.at[lo, j])
-                send(r_raw.at[lo, j], r_raw.at[lo, j], r_send.at[lo, j], r_recv.at[lo, j],
-                     device(xh, xl, y, at_z(sign), c))
-
-        @pl.when((origin // 8 == c) & (s == most))
-        def _():
-            for j in range(PIECES):
-                arrived(r_raw.at[lo, j], r_recv.at[lo, j])
-
     def pass_both(s):
-        pass_on(1, s, 8)
-        pass_on(-1, s, 7)
+        ways = [(sign, most, at_z(-sign * s)) for sign, most in ((1, 8), (-1, 7))]
+        for j in range(PIECES):
+            for sign, most, origin in ways:
+                lo = origin % 8
+
+                @pl.when((origin // 8 == c) & (s <= most))
+                def _():
+                    arrived(r_raw.at[lo, j], r_recv.at[lo, j])
+
+                    @pl.when(s < most)
+                    def _():
+                        send(r_raw.at[lo, j], r_raw.at[lo, j], r_send.at[lo, j], r_recv.at[lo, j],
+                             device(xh, xl, y, at_z(sign), c))
 
     pass_both(1)
 
@@ -178,12 +174,12 @@
                                 device(xh, g // NY, g % NY, z, (c + cc) % 2)))
     started.append(send(p_stat.at[me, c], p_stat.at[me, c], ps_send.at[0, 0], ps_recv.at[me, c],
                         device(xh, xl, y, z, other)))
+    pass_both(4)
     for k in range(1, 8):
         g = (me + k) % 8
         arrived(q_raw.at[g, c], q_recv.at[g, c])
         started.append(send(q_raw.at[g, c], q_raw.at[g, c], q_send.at[8 + k], q_recv.at[g, c],
                             device(xh, xl, y, z, other)))
-    pass_both(4)
     pass_both(5)
     for k in range(8):
         g = (me + k) % 8
@@ -246,13 +242,13 @@
         for u in range(4):
             center_pair(u)
 
-    def product(t):
+    def product(t, part_at):
         p_out, p_in, columns, los = outs[t]
-        for v in los:
+        for v in los if part_at == 0 else ():
             for j in range(PIECES):
                 r_c[v * ROWS:(v + 1) * ROWS, j * WIDTH:(j + 1) * WIDTH] = center(
                     r_raw[v, j], slice(j * WIDTH, (j + 1) * WIDTH))
-        for i in range(4):
+        for i in range(2 * part_at, 2 * part_at + 2):
             u = (turn + i) % 4
 
             @pl.when(early & leads[t])
@@ -280,9 +276,10 @@
             pass_both(s)
 
         for t in range(2):
-            @pl.when(ready[t] == s)
-            def _():
-                product(t)
+            for part_at in range(2):
+                @pl.when(jnp.minimum(ready[t] + part_at, 8) == s)
+                def _():
+                    product(t, part_at)
         return carry
 
     lax.fori_loop(LOOP_FROM, 9, step, 0)
@@ -310,6 +307,10 @@
     for t in range(2):
         for k in range(8):
             arrived(outs[t][1].at[k], o_recv.at[t, k])
+
+
+def assemble(p_in0, p_in1, upd_in, gram_ref, upd_ref):
+    upd_ref[...] = upd_in[...]
     for u in range(5):
         rows = slice(u * 16, (u + 1) * 16)
         added = [jnp.concatenate([p_in[k, rows].astype(F32) + p_in[NY + k, rows].astype(F32)
@@ -322,12 +323,13 @@
 def shards(derivatives, epsilon):
     total = derivatives.shape[0] * 128
     dma = pltpu.SemaphoreType.DMA
-    gram, upd = pl.pallas_call(
+    parts0, parts1, upd = pl.pallas_call(
         functools.partial(kernel, total),
         name="gram",
-        out_shape=(jax.ShapeDtypeStruct((ROWS, 2560), F32), jax.ShapeDtypeStruct((1, COLS), F32)),
+        out_shape=(jax.ShapeDtypeStruct((8, ROWS, SPLIT), BF16), jax.ShapeDtypeStruct((8, ROWS, 640 - SPLIT), BF16),
+                   jax.ShapeDtypeStruct((1, COLS), F32)),
         in_specs=[pl.BlockSpec(memory_space=pl.ANY), pl.BlockSpec(memory_space=pltpu.VMEM)],
-        out_specs=[pl.BlockSpec(memory_space=pltpu.VMEM)] * 2,
+        out_specs=[pl.BlockSpec(memory_space=pl.ANY)] * 2 + [pl.BlockSpec(memory_space=pltpu.VMEM)],
         scratch_shapes=[
             pltpu.VMEM((ROWS, COLS), BF16),
             pltpu.VMEM((8, 2, ROWS, COLS), BF16),
@@ -342,8 +344,6 @@
             pltpu.VMEM((1, 2 * COLS), F32),
             pltpu.VMEM((8, ROWS, SPLIT), BF16),
             pltpu.VMEM((8, ROWS, 640 - SPLIT), BF16),
-            pltpu.VMEM((8, ROWS, SPLIT), BF16),
-            pltpu.VMEM((8, ROWS, 640 - SPLIT), BF16),
             dma, dma,
             dma((16,)), dma((8, 2)),
             dma((3, SUB)), dma((8, PIECES)), dma((8, PIECES)),
@@ -353,6 +353,14 @@
         ],
         compiler_params=pltpu.CompilerParams(collective_id=0, has_side_effects=True, vmem_limit_bytes=24 << 20),
     )(derivatives, epsilon.reshape(1, ROWS))
+    gram, upd = pl.pallas_call(
+        assemble,
+        name="assemble",
+        out_shape=(jax.ShapeDtypeStruct((ROWS, 2560), F32), jax.ShapeDtypeStruct((1, COLS), F32)),
+        in_specs=[pl.BlockSpec(memory_space=pltpu.VMEM)] * 3,
+        out_specs=[pl.BlockSpec(memory_space=pltpu.VMEM)] * 2,
+        compiler_params=pltpu.CompilerParams(vmem_limit_bytes=ASSEMBLE_VMEM),
+    )(parts0, parts1, upd)
     return gram, upd.reshape(COLS)
 
 

time: 54.3 us -> 52.7 us (0.971)
  local copies, waits for them, and re-layouts: 3.01 us -> 1.53 us
    unnamed x6 -> x4, local copies, waits for them, and re-layouts: 3.01 us -> 1.53 us
    pallas_call x1, Pallas kernels: 50.4 us -> 49 us  [shards(): pl.pallas_call(functools.partial(kernel, total), name='gram', out_shape=(...]
    pallas_call x0 -> x1, Pallas kernels: none -> 1.43 us  [shards(): pl.pallas_call(assemble, name='assemble', out_shape=(jax.ShapeDtypeStruct...]
where the time goes in v4:
time: 52.7 us; the launch traced here: 52.6 us
  Pallas kernels  50.4 us (96%)
  local copies, waits for them, and re-layouts  1.53 us (3%)
  between operations  0.65 us (1%)
    pallas_call x1, Pallas kernels, shards(): pl.pallas_call(functools.partial(kernel, total), name='gram', out_shape=(...  49 us
    unnamed x4, local copies, waits for them, and re-layouts  1.53 us
    pallas_call x1, Pallas kernels, shards(): pl.pallas_call(assemble, name='assemble', out_shape=(jax.ShapeDtypeStruct...  1.43 us

profile of v4, /device:TPU:24, one launch (start us, length us, event | category | flops | bytes accessed | tf_op | source)
XLA Modules:
  0.0 52.6 jit_solution(13795873565400332860)
XLA Ops:
  0.6 0.0 copy-start.1
  0.6 0.6 %copy-done.1 = f32[80]{0:T(128)S(1)} copy-done((f32[80]{0:T(128)S(1)}, f32[80]{0:T(128)}, u32[]{:S(2)}) %copy-start.1) | copy-done | bytes 344
  1.3 0.0 copy-start
  1.3 0.9 %copy-done = bf16[80,512]{1,0:T(8,128)(2,1)S(1)} copy-done((bf16[80,512]{1,0:T(8,128)(2,1)S(1)}, bf16[80,512]{1,0:T(8,128)(2,1)}, u32[]{:S(2)}) %copy-start) | copy-done | bytes 81944
  2.2 49.0 %gram.1 = (bf16[8,80,256]{2,1,0:T(8,128)(2,1)S(1)}, bf16[8,80,384]{2,1,0:T(8,128)(2,1)S(1)}, f32[1,512]{1,0:T(1,128)S(1)}) custom-call(bf16[80,512]{1,0:T(8,128)(2,1)S(1)} %copy-done, f32[1,80]{1,0:T(1,128)S(1)} %bitcast.2), custom_call_target="tpu_custom_call" | custom-call | tf_op jit(solution)/shard_map/gram/pallas_call | solution.py:326
  51.2 1.4 %assemble.1 = (f32[80,2560]{1,0:T(8,128)}, f32[1,512]{1,0:T(1,128)}) custom-call(bf16[8,80,256]{2,1,0:T(8,128)(2,1)S(1)} %get-tuple-element.7.p_in0, bf16[8,80,384]{2,1,0:T(8,128)(2,1)S(1)} %get-tuple-element.8.p_in1, f32[1,512]{1,0:T(1,128)S(1)} %get-tuple-element.9.upd_in), custom_call_target="tpu_custom_call" | custom-call | tf_op jit(solution)/shard_map/assemble/pallas_call | solution.py:356
Async XLA Ops:
  0.6 0.7 %copy-start.1 = (f32[80]{0:T(128)S(1)}, f32[80]{0:T(128)}, u32[]{:S(2)}) copy-start(f32[80]{0:T(128)} %param.3) | copy-start | bytes 964
  1.3 0.9 %copy-start = (bf16[80,512]{1,0:T(8,128)(2,1)S(1)}, bf16[80,512]{1,0:T(8,128)(2,1)}, u32[]{:S(2)}) copy-start(bf16[80,512]{1,0:T(8,128)(2,1)} %d_hbm.1) | copy-start | bytes 245764

commit v5 on v4

--- a/solution.py
+++ b/solution.py
@@ -27,9 +27,9 @@
     return (xl * 64 + z * NY + y, xh * 2 + c)
 
 
-def kernel(total, d_hbm, eps_ref, p_in0, p_in1, upd_ref,
-           d_ref, q_raw, r_raw, q_c, r_c, stat, z_near, z_out, z_far, p_stat, mean, p_out0, p_out1,
-           d_sem, q_own, q_send, q_recv, r_src, r_send, r_recv, zn_send, zn_recv, zf_send, zf_recv,
+def kernel(total, d_ref, eps_ref, p_in0, p_in1, upd_ref,
+           q_raw, r_raw, q_c, r_c, stat, z_near, z_out, z_far, p_stat, mean, p_out0, p_out1,
+           q_own, q_send, q_recv, r_src, r_send, r_recv, zn_send, zn_recv, zf_send, zf_recv,
            ps_send, ps_recv, o_send, o_recv):
     s_at, p_at = lax.axis_index("smp"), lax.axis_index("par")
     xl, z, y = s_at // 64, (s_at // NY) % NZ, s_at % NY
@@ -38,8 +38,6 @@
     half, z_lo = z // 8, z % 8
     me = xl * NY + y
     factor = 1.0 / math.sqrt(total)
-    load = pltpu.make_async_copy(d_hbm, d_ref, d_sem)
-    load.start()
 
     def at_z(step):
         return (z + step + NZ) % NZ
@@ -67,7 +65,29 @@
             greet(device(xh, g // NY, g % NY, z, cc))
     greet(device(xh, xl, y, z, other))
 
-    load.wait()
+    pl.semaphore_wait(barrier, 8 - same.astype(jnp.int32) + len(NEAR) + 2 + 14 + 1)
+
+    started = []
+
+    def send(src, dst, s_sem, r_sem, where):
+        copy = pltpu.make_async_remote_copy(src_ref=src, dst_ref=dst, send_sem=s_sem, recv_sem=r_sem,
+                                            device_id=where, device_id_type=MESH)
+        copy.start()
+        return copy
+
+    def handle(ref, sem):
+        return pltpu.make_async_remote_copy(src_ref=ref, dst_ref=ref, send_sem=sem, recv_sem=sem,
+                                            device_id=(s_at, p_at), device_id_type=MESH)
+
+    def arrived(ref, sem):
+        handle(ref, sem).wait_recv()
+
+    for i in range(SUB):
+        for n, q in enumerate((1, -1)):
+            started.append(send(d_ref.at[:, pl.ds(i * WIDTH, WIDTH)], r_raw.at[z_lo, c * SUB + i],
+                                r_src.at[n, i], r_recv.at[z_lo, c * SUB + i],
+                                device(xh, xl, y, at_z(q), half)))
+
     d = d_ref[...].astype(F32)
     eps = eps_ref[...]
     stat[:, 0:COLS] = jnp.sum(d, axis=0, keepdims=True)
@@ -75,31 +95,8 @@
         eps, d, (((1,), (0,)), ((), ())), precision=lax.Precision.HIGHEST, preferred_element_type=F32)
     stat[:, 2 * COLS:] = jnp.broadcast_to(jnp.sum(eps, axis=1, keepdims=True), (1, 128))
 
-    pl.semaphore_wait(barrier, 8 - same.astype(jnp.int32) + len(NEAR) + 2 + 14 + 1)
-
-    started = []
-
-    def send(src, dst, s_sem, r_sem, where):
-        copy = pltpu.make_async_remote_copy(src_ref=src, dst_ref=dst, send_sem=s_sem, recv_sem=r_sem,
-                                            device_id=where, device_id_type=MESH)
-        copy.start()
-        return copy
-
-    def handle(ref, sem):
-        return pltpu.make_async_remote_copy(src_ref=ref, dst_ref=ref, send_sem=sem, recv_sem=sem,
-                                            device_id=(s_at, p_at), device_id_type=MESH)
-
-    def arrived(ref, sem):
-        handle(ref, sem).wait_recv()
-
     for n, k in enumerate(NEAR):
         started.append(send(stat, z_near.at[n], zn_send.at[n], zn_recv.at[n], device(xh, xl, y, at_z(-k), c)))
-
-    for i in range(SUB):
-        for n, q in enumerate((1, -1)):
-            started.append(send(d_ref.at[:, pl.ds(i * WIDTH, WIDTH)], r_raw.at[z_lo, c * SUB + i],
-                                r_src.at[n, i], r_recv.at[z_lo, c * SUB + i],
-                                device(xh, xl, y, at_z(q), half)))
 
     def own_copy(i):
         return pltpu.make_async_copy(d_ref.at[:, pl.ds(i * WIDTH, WIDTH)], r_raw.at[z_lo, c * SUB + i],
@@ -328,10 +325,9 @@
         name="gram",
         out_shape=(jax.ShapeDtypeStruct((8, ROWS, SPLIT), BF16), jax.ShapeDtypeStruct((8, ROWS, 640 - SPLIT), BF16),
                    jax.ShapeDtypeStruct((1, COLS), F32)),
-        in_specs=[pl.BlockSpec(memory_space=pl.ANY), pl.BlockSpec(memory_space=pltpu.VMEM)],
+        in_specs=[pl.BlockSpec(memory_space=pltpu.VMEM)] * 2,
         out_specs=[pl.BlockSpec(memory_space=pl.ANY)] * 2 + [pl.BlockSpec(memory_space=pltpu.VMEM)],
         scratch_shapes=[
-            pltpu.VMEM((ROWS, COLS), BF16),
             pltpu.VMEM((8, 2, ROWS, COLS), BF16),
             pltpu.VMEM((8, PIECES, ROWS, WIDTH), BF16),
             pltpu.VMEM((640, 2 * COLS), BF16),
@@ -344,7 +340,7 @@
             pltpu.VMEM((1, 2 * COLS), F32),
             pltpu.VMEM((8, ROWS, SPLIT), BF16),
             pltpu.VMEM((8, ROWS, 640 - SPLIT), BF16),
-            dma, dma,
+            dma,
             dma((16,)), dma((8, 2)),
             dma((3, SUB)), dma((8, PIECES)), dma((8, PIECES)),
             dma((len(NEAR),)), dma((len(NEAR),)), dma((2,)), dma((2,)),

time: 52.7 us -> 52.4 us (level)
  no operation moved by 1% of the time
where the time goes in v5:
time: 52.4 us; the launch traced here: 52.2 us
  Pallas kernels  50 us (95%)
  local copies, waits for them, and re-layouts  1.53 us (3%)
  between operations  0.65 us (1%)
    pallas_call x1, Pallas kernels, shards(): pl.pallas_call(functools.partial(kernel, total), name='gram', out_shape=(...  48.6 us
    unnamed x4, local copies, waits for them, and re-layouts  1.53 us
    pallas_call x1, Pallas kernels, shards(): pl.pallas_call(assemble, name='assemble', out_shape=(jax.ShapeDtypeStruct...  1.43 us

profile of v5, /device:TPU:24, one launch (start us, length us, event | category | flops | bytes accessed | tf_op | source)
XLA Modules:
  0.0 52.2 jit_solution(8825875719223441333)
XLA Ops:
  0.6 0.0 copy-start.1
  0.6 0.6 %copy-done.1 = f32[80]{0:T(128)S(1)} copy-done((f32[80]{0:T(128)S(1)}, f32[80]{0:T(128)}, u32[]{:S(2)}) %copy-start.1) | copy-done | bytes 344
  1.3 0.0 copy-start
  1.3 0.9 %copy-done = bf16[80,512]{1,0:T(8,128)(2,1)S(1)} copy-done((bf16[80,512]{1,0:T(8,128)(2,1)S(1)}, bf16[80,512]{1,0:T(8,128)(2,1)}, u32[]{:S(2)}) %copy-start) | copy-done | bytes 81944
  2.2 48.6 %gram.1 = (bf16[8,80,256]{2,1,0:T(8,128)(2,1)S(1)}, bf16[8,80,384]{2,1,0:T(8,128)(2,1)S(1)}, f32[1,512]{1,0:T(1,128)S(1)}) custom-call(bf16[80,512]{1,0:T(8,128)(2,1)S(1)} %copy-done, f32[1,80]{1,0:T(1,128)S(1)} %bitcast.2), custom_call_target="tpu_custom_call" | custom-call | tf_op jit(solution)/shard_map/gram/pallas_call | solution.py:323
  50.8 1.4 %assemble.1 = (f32[80,2560]{1,0:T(8,128)}, f32[1,512]{1,0:T(1,128)}) custom-call(bf16[8,80,256]{2,1,0:T(8,128)(2,1)S(1)} %get-tuple-element.7.p_in0, bf16[8,80,384]{2,1,0:T(8,128)(2,1)S(1)} %get-tuple-element.8.p_in1, f32[1,512]{1,0:T(1,128)S(1)} %get-tuple-element.9.upd_in), custom_call_target="tpu_custom_call" | custom-call | tf_op jit(solution)/shard_map/assemble/pallas_call | solution.py:352
Async XLA Ops:
  0.6 0.7 %copy-start.1 = (f32[80]{0:T(128)S(1)}, f32[80]{0:T(128)}, u32[]{:S(2)}) copy-start(f32[80]{0:T(128)} %param.3) | copy-start | bytes 964
  1.3 0.9 %copy-start = (bf16[80,512]{1,0:T(8,128)(2,1)S(1)}, bf16[80,512]{1,0:T(8,128)(2,1)}, u32[]{:S(2)}) copy-start(bf16[80,512]{1,0:T(8,128)(2,1)} %d_ref.1) | copy-start | bytes 245764

commit v6 on v5

--- a/solution.py
+++ b/solution.py
@@ -234,11 +234,6 @@
     leads = (ready[0] <= ready[1], ready[1] < ready[0])
     turn = y + 2 * xh
 
-    @pl.when(jnp.logical_not(early))
-    def _():
-        for u in range(4):
-            center_pair(u)
-
     def product(t, part_at):
         p_out, p_in, columns, los = outs[t]
         for v in los if part_at == 0 else ():
@@ -271,6 +266,11 @@
         @pl.when(s > LOOP_FROM)
         def _():
             pass_both(s)
+
+        @pl.when(jnp.logical_not(early) & (s == LOOP_FROM + 1))
+        def _():
+            for u in range(4):
+                center_pair(u)
 
         for t in range(2):
             for part_at in range(2):

time: 52.4 us -> 52.4 us (level)
  no operation moved by 1% of the time
where the time goes in v6:
time: 52.4 us; the launch traced here: 52.2 us
  Pallas kernels  50 us (95%)
  local copies, waits for them, and re-layouts  1.53 us (3%)
  between operations  0.65 us (1%)
    pallas_call x1, Pallas kernels, shards(): pl.pallas_call(functools.partial(kernel, total), name='gram', out_shape=(...  48.6 us
    unnamed x4, local copies, waits for them, and re-layouts  1.53 us
    pallas_call x1, Pallas kernels, shards(): pl.pallas_call(assemble, name='assemble', out_shape=(jax.ShapeDtypeStruct...  1.43 us

profile of v6, /device:TPU:24, one launch (start us, length us, event | category | flops | bytes accessed | tf_op | source)
XLA Modules:
  0.0 52.2 jit_solution(11659352754308589833)
XLA Ops:
  0.6 0.0 copy-start.1
  0.6 0.6 %copy-done.1 = f32[80]{0:T(128)S(1)} copy-done((f32[80]{0:T(128)S(1)}, f32[80]{0:T(128)}, u32[]{:S(2)}) %copy-start.1) | copy-done | bytes 344
  1.3 0.0 copy-start
  1.3 0.9 %copy-done = bf16[80,512]{1,0:T(8,128)(2,1)S(1)} copy-done((bf16[80,512]{1,0:T(8,128)(2,1)S(1)}, bf16[80,512]{1,0:T(8,128)(2,1)}, u32[]{:S(2)}) %copy-start) | copy-done | bytes 81944
  2.2 48.6 %gram.1 = (bf16[8,80,256]{2,1,0:T(8,128)(2,1)S(1)}, bf16[8,80,384]{2,1,0:T(8,128)(2,1)S(1)}, f32[1,512]{1,0:T(1,128)S(1)}) custom-call(bf16[80,512]{1,0:T(8,128)(2,1)S(1)} %copy-done, f32[1,80]{1,0:T(1,128)S(1)} %bitcast.2), custom_call_target="tpu_custom_call" | custom-call | tf_op jit(solution)/shard_map/gram/pallas_call | solution.py:323
  50.8 1.4 %assemble.1 = (f32[80,2560]{1,0:T(8,128)}, f32[1,512]{1,0:T(1,128)}) custom-call(bf16[8,80,256]{2,1,0:T(8,128)(2,1)S(1)} %get-tuple-element.7.p_in0, bf16[8,80,384]{2,1,0:T(8,128)(2,1)S(1)} %get-tuple-element.8.p_in1, f32[1,512]{1,0:T(1,128)S(1)} %get-tuple-element.9.upd_in), custom_call_target="tpu_custom_call" | custom-call | tf_op jit(solution)/shard_map/assemble/pallas_call | solution.py:352
Async XLA Ops:
  0.6 0.7 %copy-start.1 = (f32[80]{0:T(128)S(1)}, f32[80]{0:T(128)}, u32[]{:S(2)}) copy-start(f32[80]{0:T(128)} %param.3) | copy-start | bytes 964
  1.3 0.9 %copy-start = (bf16[80,512]{1,0:T(8,128)(2,1)S(1)}, bf16[80,512]{1,0:T(8,128)(2,1)}, u32[]{:S(2)}) copy-start(bf16[80,512]{1,0:T(8,128)(2,1)} %d_ref.1) | copy-start | bytes 245764

commit v7 on v5

--- a/solution.py
+++ b/solution.py
@@ -15,7 +15,7 @@
 SUB = 4
 WIDTH = COLS // SUB
 PIECES = 2 * SUB
-SPLIT = 256
+SPLIT = 384
 STAT = 2 * COLS + 128
 NEAR = (1, -1, 2, -2, 3, -3)
 FAR = 6
@@ -217,7 +217,7 @@
             arrived(r_raw.at[z_lo, j], r_recv.at[z_lo, j])
 
     slot = xh * NY + y
-    outs = ((p_out0, p_in0, slice(0, SPLIT), range(4)), (p_out1, p_in1, slice(SPLIT, 640), range(3, 8)))
+    outs = ((p_out0, p_in0, slice(0, SPLIT), range(5)), (p_out1, p_in1, slice(SPLIT, 640), range(4, 8)))
 
     def out_is_me(g):
         return same & (g == me)

time: 52.4 us -> 52.8 us (level)
  no operation moved by 1% of the time
where the time goes in v7:
time: 52.8 us; the launch traced here: 52.6 us
  Pallas kernels  50.4 us (95%)
  local copies, waits for them, and re-layouts  1.53 us (3%)
  between operations  0.65 us (1%)
    pallas_call x1, Pallas kernels, shards(): pl.pallas_call(functools.partial(kernel, total), name='gram', out_shape=(...  49 us
    unnamed x4, local copies, waits for them, and re-layouts  1.53 us
    pallas_call x1, Pallas kernels, shards(): pl.pallas_call(assemble, name='assemble', out_shape=(jax.ShapeDtypeStruct...  1.43 us

profile of v7, /device:TPU:24, one launch (start us, length us, event | category | flops | bytes accessed | tf_op | source)
XLA Modules:
  0.0 52.6 jit_solution(3537989439142312539)
XLA Ops:
  0.6 0.0 copy-start.1
  0.6 0.6 %copy-done.1 = f32[80]{0:T(128)S(1)} copy-done((f32[80]{0:T(128)S(1)}, f32[80]{0:T(128)}, u32[]{:S(2)}) %copy-start.1) | copy-done | bytes 344
  1.3 0.0 copy-start
  1.3 0.9 %copy-done = bf16[80,512]{1,0:T(8,128)(2,1)S(1)} copy-done((bf16[80,512]{1,0:T(8,128)(2,1)S(1)}, bf16[80,512]{1,0:T(8,128)(2,1)}, u32[]{:S(2)}) %copy-start) | copy-done | bytes 81944
  2.2 49.0 %gram.1 = (bf16[8,80,384]{2,1,0:T(8,128)(2,1)S(1)}, bf16[8,80,256]{2,1,0:T(8,128)(2,1)S(1)}, f32[1,512]{1,0:T(1,128)S(1)}) custom-call(bf16[80,512]{1,0:T(8,128)(2,1)S(1)} %copy-done, f32[1,80]{1,0:T(1,128)S(1)} %bitcast.2), custom_call_target="tpu_custom_call" | custom-call | tf_op jit(solution)/shard_map/gram/pallas_call | solution.py:323
  51.2 1.4 %assemble.1 = (f32[80,2560]{1,0:T(8,128)}, f32[1,512]{1,0:T(1,128)}) custom-call(bf16[8,80,384]{2,1,0:T(8,128)(2,1)S(1)} %get-tuple-element.7.p_in0, bf16[8,80,256]{2,1,0:T(8,128)(2,1)S(1)} %get-tuple-element.8.p_in1, f32[1,512]{1,0:T(1,128)S(1)} %get-tuple-element.9.upd_in), custom_call_target="tpu_custom_call" | custom-call | tf_op jit(solution)/shard_map/assemble/pallas_call | solution.py:352
Async XLA Ops:
  0.6 0.7 %copy-start.1 = (f32[80]{0:T(128)S(1)}, f32[80]{0:T(128)}, u32[]{:S(2)}) copy-start(f32[80]{0:T(128)} %param.3) | copy-start | bytes 964
  1.3 0.9 %copy-start = (bf16[80,512]{1,0:T(8,128)(2,1)S(1)}, bf16[80,512]{1,0:T(8,128)(2,1)}, u32[]{:S(2)}) copy-start(bf16[80,512]{1,0:T(8,128)(2,1)} %d_ref.1) | copy-start | bytes 245764
